TPU v7x, 512 devices: a whole 4x4x16 slice. The times are simulated.
512 devices in a mesh: row: 8 (over y, z_hi), col: 16 (over z_lo, core), rep: 4 (over x).
Axes of the slice: x: 4, y: 4, z: 16 (z_hi: 2, z_lo: 8; z = z_hi * 8 + z_lo), core: 2. Of those that a mesh axis runs over, the one named last changes fastest.
Arguments:
- amplitudes: float32 [18432, 18432], P('row', ('col', 'rep')), may hold values from -0.046875 to 0.046875
- cycle_ints: float32 [18432, 1152], P(('col', 'rep'), 'row'), may hold values from -16 to 16
Outputs:
- cycle_term: float32 [18432, 1152], P(('row', 'rep'), 'col')
All inputs are finite; a program needn't handle non-finite values.
Results may differ from a plain program's by a relative error of at most 0.0002.
Values sent between devices are 32-bit elements; how exact they have to be, the bound alone decides.
A program may use at most 64 MiB of HBM per device.

v0:
```python
import jax
import jax.numpy as jnp
from jax import lax
from jax.sharding import PartitionSpec as P


def passed_along(x, axis, by):
    devices = lax.axis_size(axis)
    return lax.ppermute(x, axis, [(i, (i + by) % devices) for i in range(devices)])


def per_device(amplitudes, cycle_ints):
    n_col = lax.axis_size("col")
    full_ints = lax.all_gather(cycle_ints, "row", axis=1, tiled=True)
    width = full_ints.shape[1] // n_col
    here = lax.axis_index("col")
    n_rows = amplitudes.shape[0]

    def product(block, offset, count):
        columns = lax.dynamic_slice_in_dim(full_ints, block * width + offset, count, 1)
        return jnp.dot(
            amplitudes, columns, precision=lax.Precision.HIGHEST, preferred_element_type=jnp.float32
        )

    def advance(step, partial_sum):
        block = (here - step) % n_col
        partial_sum = partial_sum + product(block, 0, width)
        return passed_along(partial_sum, "col", 1)

    totals = lax.fori_loop(0, n_col, advance, jnp.zeros((n_rows, width), jnp.float32))
    return lax.psum_scatter(totals, "rep", scatter_dimension=0, tiled=True)


def solution(mesh):
    return jax.shard_map(
        per_device,
        mesh=mesh,
        in_specs=(P("row", ("col", "rep")), P(("col", "rep"), "row")),
        out_specs=P(("row", "rep"), "col"),
        check_vma=False,
    )
```

profile of v0, /device:TPU:16, one launch (start us, length us, event | category | flops | bytes accessed | tf_op | source)
XLA Modules:
  0.0 518.8 jit_solution(9716333784777481202)
XLA Ops:
  7.3 116.6 %all-gather.2.cloned.1.call-done = f32[288,1152]{0,1:T(8,128)} async-done(((f32[288,144]{0,1:T(8,128)}), f32[288,1152]{0,1:T(8,128)}) %all-gather.2.cloned.1.call-update) | async-done | bytes 1327120 | tf_op jit(solution)/shard_map/all_gather | solution.py:14
  123.9 360.8 %while.15 = (s32[]{:T(128)}, f32[2304,72]{0,1:T(8,128)S(1)}, s32[]{:T(128)}, f32[288,1152]{0,1:T(8,128)}, f32[2304,288]{0,1:T(8,128)}, /*index=5*/s32[]{:T(128)}...) while((s32[]{:T(128)}, f32[2304,72]{0,1:T(8,128)S(1)}, s32[]{:T(128)}, ...), condition=%wide.region_1.2_spmd, body=%wide.region_0.1_spmd.sunk | while | flops 573474816 | bytes 6746432 | solution.py:30
  124.0 3.9 fusion.9
  127.9 1.9 collective-permute-start
  129.8 16.7 %collective-permute-done = f32[2304,72]{0,1:T(8,128)S(1)} collective-permute-done((f32[2304,72]{0,1:T(8,128)S(1)}, f32[2304,72]{0,1:T(8,128)S(1)}, u32[]{:S(2)}, u32[]{:S(2)}) %collective-permute-start) | collective-permute-done | bytes 663584 | tf_op jit(solution)/shard_map/while/body/eval_jaxpr/ppermute | solution.py:9
  146.5 3.9 fusion.9
  150.5 1.9 collective-permute-start
  152.4 16.7 %collective-permute-done = f32[2304,72]{0,1:T(8,128)S(1)} collective-permute-done((f32[2304,72]{0,1:T(8,128)S(1)}, f32[2304,72]{0,1:T(8,128)S(1)}, u32[]{:S(2)}, u32[]{:S(2)}) %collective-permute-start) | collective-permute-done | bytes 663584 | tf_op jit(solution)/shard_map/while/body/eval_jaxpr/ppermute | solution.py:9
  169.1 3.9 fusion.9
  173.0 1.9 collective-permute-start
  174.9 16.7 %collective-permute-done = f32[2304,72]{0,1:T(8,128)S(1)} collective-permute-done((f32[2304,72]{0,1:T(8,128)S(1)}, f32[2304,72]{0,1:T(8,128)S(1)}, u32[]{:S(2)}, u32[]{:S(2)}) %collective-permute-start) | collective-permute-done | bytes 663584 | tf_op jit(solution)/shard_map/while/body/eval_jaxpr/ppermute | solution.py:9
  191.6 3.9 fusion.9
  195.5 1.9 collective-permute-start
  197.5 16.7 %collective-permute-done = f32[2304,72]{0,1:T(8,128)S(1)} collective-permute-done((f32[2304,72]{0,1:T(8,128)S(1)}, f32[2304,72]{0,1:T(8,128)S(1)}, u32[]{:S(2)}, u32[]{:S(2)}) %collective-permute-start) | collective-permute-done | bytes 663584 | tf_op jit(solution)/shard_map/while/body/eval_jaxpr/ppermute | solution.py:9
  214.1 3.9 fusion.9
  218.1 1.9 collective-permute-start
  220.0 16.7 %collective-permute-done = f32[2304,72]{0,1:T(8,128)S(1)} collective-permute-done((f32[2304,72]{0,1:T(8,128)S(1)}, f32[2304,72]{0,1:T(8,128)S(1)}, u32[]{:S(2)}, u32[]{:S(2)}) %collective-permute-start) | collective-permute-done | bytes 663584 | tf_op jit(solution)/shard_map/while/body/eval_jaxpr/ppermute | solution.py:9
  236.7 3.9 fusion.9
  240.6 1.9 collective-permute-start
  242.6 16.7 %collective-permute-done = f32[2304,72]{0,1:T(8,128)S(1)} collective-permute-done((f32[2304,72]{0,1:T(8,128)S(1)}, f32[2304,72]{0,1:T(8,128)S(1)}, u32[]{:S(2)}, u32[]{:S(2)}) %collective-permute-start) | collective-permute-done | bytes 663584 | tf_op jit(solution)/shard_map/while/body/eval_jaxpr/ppermute | solution.py:9
  259.2 3.9 fusion.9
  263.2 1.9 collective-permute-start
  265.1 16.7 %collective-permute-done = f32[2304,72]{0,1:T(8,128)S(1)} collective-permute-done((f32[2304,72]{0,1:T(8,128)S(1)}, f32[2304,72]{0,1:T(8,128)S(1)}, u32[]{:S(2)}, u32[]{:S(2)}) %collective-permute-start) | collective-permute-done | bytes 663584 | tf_op jit(solution)/shard_map/while/body/eval_jaxpr/ppermute | solution.py:9
  281.8 3.9 fusion.9
  285.7 1.9 collective-permute-start
  287.7 16.7 %collective-permute-done = f32[2304,72]{0,1:T(8,128)S(1)} collective-permute-done((f32[2304,72]{0,1:T(8,128)S(1)}, f32[2304,72]{0,1:T(8,128)S(1)}, u32[]{:S(2)}, u32[]{:S(2)}) %collective-permute-start) | collective-permute-done | bytes 663584 | tf_op jit(solution)/shard_map/while/body/eval_jaxpr/ppermute | solution.py:9
  304.3 3.9 fusion.9
  308.3 1.9 collective-permute-start
  310.2 16.7 %collective-permute-done = f32[2304,72]{0,1:T(8,128)S(1)} collective-permute-done((f32[2304,72]{0,1:T(8,128)S(1)}, f32[2304,72]{0,1:T(8,128)S(1)}, u32[]{:S(2)}, u32[]{:S(2)}) %collective-permute-start) | collective-permute-done | bytes 663584 | tf_op jit(solution)/shard_map/while/body/eval_jaxpr/ppermute | solution.py:9
  326.9 3.9 fusion.9
  330.8 1.9 collective-permute-start
  332.8 16.7 %collective-permute-done = f32[2304,72]{0,1:T(8,128)S(1)} collective-permute-done((f32[2304,72]{0,1:T(8,128)S(1)}, f32[2304,72]{0,1:T(8,128)S(1)}, u32[]{:S(2)}, u32[]{:S(2)}) %collective-permute-start) | collective-permute-done | bytes 663584 | tf_op jit(solution)/shard_map/while/body/eval_jaxpr/ppermute | solution.py:9
  349.4 3.9 fusion.9
  353.4 1.9 collective-permute-start
  355.3 16.7 %collective-permute-done = f32[2304,72]{0,1:T(8,128)S(1)} collective-permute-done((f32[2304,72]{0,1:T(8,128)S(1)}, f32[2304,72]{0,1:T(8,128)S(1)}, u32[]{:S(2)}, u32[]{:S(2)}) %collective-permute-start) | collective-permute-done | bytes 663584 | tf_op jit(solution)/shard_map/while/body/eval_jaxpr/ppermute | solution.py:9
  372.0 3.9 fusion.9
  375.9 1.9 collective-permute-start
  377.8 16.7 %collective-permute-done = f32[2304,72]{0,1:T(8,128)S(1)} collective-permute-done((f32[2304,72]{0,1:T(8,128)S(1)}, f32[2304,72]{0,1:T(8,128)S(1)}, u32[]{:S(2)}, u32[]{:S(2)}) %collective-permute-start) | collective-permute-done | bytes 663584 | tf_op jit(solution)/shard_map/while/body/eval_jaxpr/ppermute | solution.py:9
  394.5 3.9 fusion.9
  400.4 16.7 %collective-permute-done = f32[2304,72]{0,1:T(8,128)S(1)} collective-permute-done((f32[2304,72]{0,1:T(8,128)S(1)}, f32[2304,72]{0,1:T(8,128)S(1)}, u32[]{:S(2)}, u32[]{:S(2)}) %collective-permute-start) | collective-permute-done | bytes 663584 | tf_op jit(solution)/shard_map/while/body/eval_jaxpr/ppermute | solution.py:9
  417.1 3.9 fusion.9
  422.9 16.7 %collective-permute-done = f32[2304,72]{0,1:T(8,128)S(1)} collective-permute-done((f32[2304,72]{0,1:T(8,128)S(1)}, f32[2304,72]{0,1:T(8,128)S(1)}, u32[]{:S(2)}, u32[]{:S(2)}) %collective-permute-start) | collective-permute-done | bytes 663584 | tf_op jit(solution)/shard_map/while/body/eval_jaxpr/ppermute | solution.py:9
  439.6 3.9 fusion.9
  443.6 1.9 collective-permute-start
  445.5 16.7 %collective-permute-done = f32[2304,72]{0,1:T(8,128)S(1)} collective-permute-done((f32[2304,72]{0,1:T(8,128)S(1)}, f32[2304,72]{0,1:T(8,128)S(1)}, u32[]{:S(2)}, u32[]{:S(2)}) %collective-permute-start) | collective-permute-done | bytes 663584 | tf_op jit(solution)/shard_map/while/body/eval_jaxpr/ppermute | solution.py:9
  462.1 3.9 fusion.9
  468.0 16.7 %collective-permute-done = f32[2304,72]{0,1:T(8,128)S(1)} collective-permute-done((f32[2304,72]{0,1:T(8,128)S(1)}, f32[2304,72]{0,1:T(8,128)S(1)}, u32[]{:S(2)}, u32[]{:S(2)}) %collective-permute-start) | collective-permute-done | bytes 663584 | tf_op jit(solution)/shard_map/while/body/eval_jaxpr/ppermute | solution.py:9
  486.1 24.0 %reduce-scatter.4.cloned.1.call-done = f32[576,72]{1,0:T(8,128)} async-done(((f32[2304,72]{1,0:T(8,128)}), f32[576,72]{1,0:T(8,128)}) %reduce-scatter.4.cloned.1.call-update) | async-done | bytes 165904
  (10 shorter events, 9.7 us)
Async XLA Ops:
  6.5 117.3 %all-gather.2.cloned.1.call-start = ((), (), s32[]{:S(2)}) async-start(), calls=%async_computation.1 | async-start | bytes 1990656 | tf_op jit(solution)/shard_map/all_gather | solution.py:14
  7.3 502.9 %reduce-scatter.4.cloned.1.call-start = ((), (), s32[]{:S(2)}) async-start(), calls=%async_computation.2 | async-start | bytes 1474560
  127.9 18.6 %collective-permute-start = (f32[2304,72]{0,1:T(8,128)S(1)}, f32[2304,72]{0,1:T(8,128)S(1)}, u32[]{:S(2)}, u32[]{:S(2)}) collective-permute-start(f32[2304,72]{0,1:T(8,128)S(1)} %fusion.9), channel_id=1, source_target_pairs={{0,4},{4,8},{8,12},{12,16},{16,20},{20,24},{24,28},{28,32},{32,36}... | collective-permute-start | bytes 1990664 | tf_op jit(solution)/shard_map/while/body/eval_jaxpr/ppermute | solution.py:9
  150.5 18.6 %collective-permute-start = (f32[2304,72]{0,1:T(8,128)S(1)}, f32[2304,72]{0,1:T(8,128)S(1)}, u32[]{:S(2)}, u32[]{:S(2)}) collective-permute-start(f32[2304,72]{0,1:T(8,128)S(1)} %fusion.9), channel_id=1, source_target_pairs={{0,4},{4,8},{8,12},{12,16},{16,20},{20,24},{24,28},{28,32},{32,36}... | collective-permute-start | bytes 1990664 | tf_op jit(solution)/shard_map/while/body/eval_jaxpr/ppermute | solution.py:9
  173.0 18.6 %collective-permute-start = (f32[2304,72]{0,1:T(8,128)S(1)}, f32[2304,72]{0,1:T(8,128)S(1)}, u32[]{:S(2)}, u32[]{:S(2)}) collective-permute-start(f32[2304,72]{0,1:T(8,128)S(1)} %fusion.9), channel_id=1, source_target_pairs={{0,4},{4,8},{8,12},{12,16},{16,20},{20,24},{24,28},{28,32},{32,36}... | collective-permute-start | bytes 1990664 | tf_op jit(solution)/shard_map/while/body/eval_jaxpr/ppermute | solution.py:9
  195.5 18.6 %collective-permute-start = (f32[2304,72]{0,1:T(8,128)S(1)}, f32[2304,72]{0,1:T(8,128)S(1)}, u32[]{:S(2)}, u32[]{:S(2)}) collective-permute-start(f32[2304,72]{0,1:T(8,128)S(1)} %fusion.9), channel_id=1, source_target_pairs={{0,4},{4,8},{8,12},{12,16},{16,20},{20,24},{24,28},{28,32},{32,36}... | collective-permute-start | bytes 1990664 | tf_op jit(solution)/shard_map/while/body/eval_jaxpr/ppermute | solution.py:9
  218.1 18.6 %collective-permute-start = (f32[2304,72]{0,1:T(8,128)S(1)}, f32[2304,72]{0,1:T(8,128)S(1)}, u32[]{:S(2)}, u32[]{:S(2)}) collective-permute-start(f32[2304,72]{0,1:T(8,128)S(1)} %fusion.9), channel_id=1, source_target_pairs={{0,4},{4,8},{8,12},{12,16},{16,20},{20,24},{24,28},{28,32},{32,36}... | collective-permute-start | bytes 1990664 | tf_op jit(solution)/shard_map/while/body/eval_jaxpr/ppermute | solution.py:9
  240.6 18.6 %collective-permute-start = (f32[2304,72]{0,1:T(8,128)S(1)}, f32[2304,72]{0,1:T(8,128)S(1)}, u32[]{:S(2)}, u32[]{:S(2)}) collective-permute-start(f32[2304,72]{0,1:T(8,128)S(1)} %fusion.9), channel_id=1, source_target_pairs={{0,4},{4,8},{8,12},{12,16},{16,20},{20,24},{24,28},{28,32},{32,36}... | collective-permute-start | bytes 1990664 | tf_op jit(solution)/shard_map/while/body/eval_jaxpr/ppermute | solution.py:9
  263.2 18.6 %collective-permute-start = (f32[2304,72]{0,1:T(8,128)S(1)}, f32[2304,72]{0,1:T(8,128)S(1)}, u32[]{:S(2)}, u32[]{:S(2)}) collective-permute-start(f32[2304,72]{0,1:T(8,128)S(1)} %fusion.9), channel_id=1, source_target_pairs={{0,4},{4,8},{8,12},{12,16},{16,20},{20,24},{24,28},{28,32},{32,36}... | collective-permute-start | bytes 1990664 | tf_op jit(solution)/shard_map/while/body/eval_jaxpr/ppermute | solution.py:9
  285.7 18.6 %collective-permute-start = (f32[2304,72]{0,1:T(8,128)S(1)}, f32[2304,72]{0,1:T(8,128)S(1)}, u32[]{:S(2)}, u32[]{:S(2)}) collective-permute-start(f32[2304,72]{0,1:T(8,128)S(1)} %fusion.9), channel_id=1, source_target_pairs={{0,4},{4,8},{8,12},{12,16},{16,20},{20,24},{24,28},{28,32},{32,36}... | collective-permute-start | bytes 1990664 | tf_op jit(solution)/shard_map/while/body/eval_jaxpr/ppermute | solution.py:9
  308.3 18.6 %collective-permute-start = (f32[2304,72]{0,1:T(8,128)S(1)}, f32[2304,72]{0,1:T(8,128)S(1)}, u32[]{:S(2)}, u32[]{:S(2)}) collective-permute-start(f32[2304,72]{0,1:T(8,128)S(1)} %fusion.9), channel_id=1, source_target_pairs={{0,4},{4,8},{8,12},{12,16},{16,20},{20,24},{24,28},{28,32},{32,36}... | collective-permute-start | bytes 1990664 | tf_op jit(solution)/shard_map/while/body/eval_jaxpr/ppermute | solution.py:9
  330.8 18.6 %collective-permute-start = (f32[2304,72]{0,1:T(8,128)S(1)}, f32[2304,72]{0,1:T(8,128)S(1)}, u32[]{:S(2)}, u32[]{:S(2)}) collective-permute-start(f32[2304,72]{0,1:T(8,128)S(1)} %fusion.9), channel_id=1, source_target_pairs={{0,4},{4,8},{8,12},{12,16},{16,20},{20,24},{24,28},{28,32},{32,36}... | collective-permute-start | bytes 1990664 | tf_op jit(solution)/shard_map/while/body/eval_jaxpr/ppermute | solution.py:9
  353.4 18.6 %collective-permute-start = (f32[2304,72]{0,1:T(8,128)S(1)}, f32[2304,72]{0,1:T(8,128)S(1)}, u32[]{:S(2)}, u32[]{:S(2)}) collective-permute-start(f32[2304,72]{0,1:T(8,128)S(1)} %fusion.9), channel_id=1, source_target_pairs={{0,4},{4,8},{8,12},{12,16},{16,20},{20,24},{24,28},{28,32},{32,36}... | collective-permute-start | bytes 1990664 | tf_op jit(solution)/shard_map/while/body/eval_jaxpr/ppermute | solution.py:9
  375.9 18.6 %collective-permute-start = (f32[2304,72]{0,1:T(8,128)S(1)}, f32[2304,72]{0,1:T(8,128)S(1)}, u32[]{:S(2)}, u32[]{:S(2)}) collective-permute-start(f32[2304,72]{0,1:T(8,128)S(1)} %fusion.9), channel_id=1, source_target_pairs={{0,4},{4,8},{8,12},{12,16},{16,20},{20,24},{24,28},{28,32},{32,36}... | collective-permute-start | bytes 1990664 | tf_op jit(solution)/shard_map/while/body/eval_jaxpr/ppermute | solution.py:9
  398.5 18.6 %collective-permute-start = (f32[2304,72]{0,1:T(8,128)S(1)}, f32[2304,72]{0,1:T(8,128)S(1)}, u32[]{:S(2)}, u32[]{:S(2)}) collective-permute-start(f32[2304,72]{0,1:T(8,128)S(1)} %fusion.9), channel_id=1, source_target_pairs={{0,4},{4,8},{8,12},{12,16},{16,20},{20,24},{24,28},{28,32},{32,36}... | collective-permute-start | bytes 1990664 | tf_op jit(solution)/shard_map/while/body/eval_jaxpr/ppermute | solution.py:9
  421.0 18.6 %collective-permute-start = (f32[2304,72]{0,1:T(8,128)S(1)}, f32[2304,72]{0,1:T(8,128)S(1)}, u32[]{:S(2)}, u32[]{:S(2)}) collective-permute-start(f32[2304,72]{0,1:T(8,128)S(1)} %fusion.9), channel_id=1, source_target_pairs={{0,4},{4,8},{8,12},{12,16},{16,20},{20,24},{24,28},{28,32},{32,36}... | collective-permute-start | bytes 1990664 | tf_op jit(solution)/shard_map/while/body/eval_jaxpr/ppermute | solution.py:9
  443.6 18.6 %collective-permute-start = (f32[2304,72]{0,1:T(8,128)S(1)}, f32[2304,72]{0,1:T(8,128)S(1)}, u32[]{:S(2)}, u32[]{:S(2)}) collective-permute-start(f32[2304,72]{0,1:T(8,128)S(1)} %fusion.9), channel_id=1, source_target_pairs={{0,4},{4,8},{8,12},{12,16},{16,20},{20,24},{24,28},{28,32},{32,36}... | collective-permute-start | bytes 1990664 | tf_op jit(solution)/shard_map/while/body/eval_jaxpr/ppermute | solution.py:9
  466.1 18.6 %collective-permute-start = (f32[2304,72]{0,1:T(8,128)S(1)}, f32[2304,72]{0,1:T(8,128)S(1)}, u32[]{:S(2)}, u32[]{:S(2)}) collective-permute-start(f32[2304,72]{0,1:T(8,128)S(1)} %fusion.9), channel_id=1, source_target_pairs={{0,4},{4,8},{8,12},{12,16},{16,20},{20,24},{24,28},{28,32},{32,36}... | collective-permute-start | bytes 1990664 | tf_op jit(solution)/shard_map/while/body/eval_jaxpr/ppermute | solution.py:9
Sparse Core Ops, SparseCore 0:
  10.5 113.2 all-gather.1
  486.2 23.8 reduce-scatter.3
where the time goes:
time: 520 us; the launch traced here: 519 us
  waiting for transfers between devices  408 us (78%)
  matrix products  63.1 us (12%)
  starting transfers between devices  30.8 us (6%)
  between operations  13.4 us (3%)
    ppermute x16, waiting for transfers between devices, passed_along(): lax.ppermute(x, axis, [(i, (i + by) % devices) for i in range(devices)])  267 us
    all_gather x1, waiting for transfers between devices, per_device(): full_ints = lax.all_gather(cycle_ints, 'row', axis=1, tiled=True)  117 us
    dot_general x16, matrix products, product(): jnp.dot(amplitudes, columns, precision=lax.Precision.HIGHEST, preferred_e...  63.1 us
    ppermute x16, starting transfers between devices, passed_along(): lax.ppermute(x, axis, [(i, (i + by) % devices) for i in range(devices)])  30.7 us
    unnamed x3, waiting for transfers between devices  24.8 us
  transfers between devices with their start and end apart: 18, of which 18 were waited for; matrix products, arithmetic and copies ran while one was open for 0% of the time, Pallas kernels for 0%

commit v1 on v0

--- a/solution.py
+++ b/solution.py
@@ -11,7 +11,8 @@
 
 def per_device(amplitudes, cycle_ints):
     n_col = lax.axis_size("col")
-    full_ints = lax.all_gather(cycle_ints, "row", axis=1, tiled=True)
+    piece_next = lax.all_to_all(jnp.stack([cycle_ints] * lax.axis_size("row"), axis=0), "row", 0, 0)
+    full_ints = jnp.concatenate(piece_next, axis=1)
     width = full_ints.shape[1] // n_col
     here = lax.axis_index("col")
     n_rows = amplitudes.shape[0]

time: 520 us -> 496 us (0.954)
  the two profiles are of different devices: /device:TPU:16 before, /device:TPU:8 now
where the time goes in v1:
time: 496 us; the launch traced here: 494 us
  waiting for transfers between devices  358 us (72%)
  matrix products  61.7 us (12%)
  starting transfers between devices  55.3 us (11%)
  between operations  13.4 us (3%)
  local copies, waits for them, and re-layouts  5.47 us (1%)
    ppermute x16, waiting for transfers between devices, passed_along(): lax.ppermute(x, axis, [(i, (i + by) % devices) for i in range(devices)])  291 us
    dot_general x16, matrix products, product(): jnp.dot(amplitudes, columns, precision=lax.Precision.HIGHEST, preferred_e...  61.7 us
    all_to_all x1, waiting for transfers between devices, per_device(): lax.all_to_all(jnp.stack([cycle_ints] * lax.axis_size('row'), axis=0), 'r...  43.8 us
    ppermute x16, starting transfers between devices, passed_along(): lax.ppermute(x, axis, [(i, (i + by) % devices) for i in range(devices)])  36.8 us
    unnamed x2, waiting for transfers between devices  23.6 us
    all_to_all x1, starting transfers between devices, per_device(): lax.all_to_all(jnp.stack([cycle_ints] * lax.axis_size('row'), axis=0), 'r...  18.4 us
  transfers between devices with their start and end apart: 18, of which 18 were waited for; matrix products, arithmetic and copies ran while one was open for 0% of the time, Pallas kernels for 0%

profile of v1, /device:TPU:8, one launch (start us, length us, event | category | flops | bytes accessed | tf_op | source)
XLA Modules:
  0.0 494.4 jit_solution(16039151856179959178)
XLA Ops:
  6.5 2.2 stack.2
  8.8 18.4 %all-to-all-start = ((f32[8,288,144]{1,2,0:T(8,128)}), f32[8,288,144]{1,2,0:T(8,128)}, u32[]{:S(2)}, u32[]{:S(2)}) async-start(f32[8,288,144]{1,2,0:T(8,128)} %stack.2), calls=%async_computation | async-start | bytes 3538944 | tf_op jit(solution)/shard_map/all_to_all | solution.py:14
  27.2 43.8 %all-to-all-done = f32[8,288,144]{1,2,0:T(8,128)} async-done(((f32[8,288,144]{1,2,0:T(8,128)}), f32[8,288,144]{1,2,0:T(8,128)}, u32[]{:S(2)}, u32[]{:S(2)}) %all-to-all-start) | async-done | bytes 1327136 | tf_op jit(solution)/shard_map/all_to_all | solution.py:14
  71.1 389.8 %while.15 = (s32[]{:T(128)}, f32[2304,72]{0,1:T(8,128)S(1)}, s32[]{:T(128)}, f32[288,1152]{0,1:T(8,128)}, f32[2304,288]{0,1:T(8,128)S(1)}, /*index=5*/s32[]{:T(1...) while((s32[]{:T(128)}, f32[2304,72]{0,1:T(8,128)S(1)}, s32[]{:T(128)}, ...), condition=%wide.region_1.2_spmd, body=%wide.region_0.1_spmd.sunk | while | flops 573474816 | bytes 6746432 | solution.py:31
  71.1 3.9 fusion.9
  75.0 1.9 collective-permute-start
  76.9 44.2 %collective-permute-done = f32[2304,72]{0,1:T(8,128)S(1)} collective-permute-done((f32[2304,72]{0,1:T(8,128)}, f32[2304,72]{0,1:T(8,128)S(1)}, u32[]{:S(2)}, u32[]{:S(2)}) %collective-permute-start) | collective-permute-done | bytes 663584 | tf_op jit(solution)/shard_map/while/body/eval_jaxpr/ppermute | solution.py:9
  121.1 3.9 fusion.9
  124.9 8.2 %collective-permute-start = (f32[2304,72]{0,1:T(8,128)}, f32[2304,72]{0,1:T(8,128)S(1)}, u32[]{:S(2)}, u32[]{:S(2)}) collective-permute-start(f32[2304,72]{0,1:T(8,128)} %fusion.9), channel_id=1, source_target_pairs={{0,4},{4,8},{8,12},{12,16},{16,20},{20,24},{24,28},{28,32},{32,36}... | collective-permute-start | bytes 1990664 | tf_op jit(solution)/shard_map/while/body/eval_jaxpr/ppermute | solution.py:9
  133.1 10.6 %collective-permute-done = f32[2304,72]{0,1:T(8,128)S(1)} collective-permute-done((f32[2304,72]{0,1:T(8,128)}, f32[2304,72]{0,1:T(8,128)S(1)}, u32[]{:S(2)}, u32[]{:S(2)}) %collective-permute-start) | collective-permute-done | bytes 663584 | tf_op jit(solution)/shard_map/while/body/eval_jaxpr/ppermute | solution.py:9
  143.7 3.9 fusion.9
  149.5 16.9 %collective-permute-done = f32[2304,72]{0,1:T(8,128)S(1)} collective-permute-done((f32[2304,72]{0,1:T(8,128)}, f32[2304,72]{0,1:T(8,128)S(1)}, u32[]{:S(2)}, u32[]{:S(2)}) %collective-permute-start) | collective-permute-done | bytes 663584 | tf_op jit(solution)/shard_map/while/body/eval_jaxpr/ppermute | solution.py:9
  166.4 3.9 fusion.9
  170.2 1.9 collective-permute-start
  172.1 16.9 %collective-permute-done = f32[2304,72]{0,1:T(8,128)S(1)} collective-permute-done((f32[2304,72]{0,1:T(8,128)}, f32[2304,72]{0,1:T(8,128)S(1)}, u32[]{:S(2)}, u32[]{:S(2)}) %collective-permute-start) | collective-permute-done | bytes 663584 | tf_op jit(solution)/shard_map/while/body/eval_jaxpr/ppermute | solution.py:9
  189.0 3.9 fusion.9
  194.8 16.9 %collective-permute-done = f32[2304,72]{0,1:T(8,128)S(1)} collective-permute-done((f32[2304,72]{0,1:T(8,128)}, f32[2304,72]{0,1:T(8,128)S(1)}, u32[]{:S(2)}, u32[]{:S(2)}) %collective-permute-start) | collective-permute-done | bytes 663584 | tf_op jit(solution)/shard_map/while/body/eval_jaxpr/ppermute | solution.py:9
  211.7 3.9 fusion.9
  215.5 1.9 collective-permute-start
  217.4 16.9 %collective-permute-done = f32[2304,72]{0,1:T(8,128)S(1)} collective-permute-done((f32[2304,72]{0,1:T(8,128)}, f32[2304,72]{0,1:T(8,128)S(1)}, u32[]{:S(2)}, u32[]{:S(2)}) %collective-permute-start) | collective-permute-done | bytes 663584 | tf_op jit(solution)/shard_map/while/body/eval_jaxpr/ppermute | solution.py:9
  234.3 3.9 fusion.9
  238.2 1.9 collective-permute-start
  240.1 16.9 %collective-permute-done = f32[2304,72]{0,1:T(8,128)S(1)} collective-permute-done((f32[2304,72]{0,1:T(8,128)}, f32[2304,72]{0,1:T(8,128)S(1)}, u32[]{:S(2)}, u32[]{:S(2)}) %collective-permute-start) | collective-permute-done | bytes 663584 | tf_op jit(solution)/shard_map/while/body/eval_jaxpr/ppermute | solution.py:9
  257.0 3.9 fusion.9
  260.8 1.9 collective-permute-start
  262.8 16.9 %collective-permute-done = f32[2304,72]{0,1:T(8,128)S(1)} collective-permute-done((f32[2304,72]{0,1:T(8,128)}, f32[2304,72]{0,1:T(8,128)S(1)}, u32[]{:S(2)}, u32[]{:S(2)}) %collective-permute-start) | collective-permute-done | bytes 663584 | tf_op jit(solution)/shard_map/while/body/eval_jaxpr/ppermute | solution.py:9
  279.6 3.9 fusion.9
  283.5 1.9 collective-permute-start
  285.4 16.9 %collective-permute-done = f32[2304,72]{0,1:T(8,128)S(1)} collective-permute-done((f32[2304,72]{0,1:T(8,128)}, f32[2304,72]{0,1:T(8,128)S(1)}, u32[]{:S(2)}, u32[]{:S(2)}) %collective-permute-start) | collective-permute-done | bytes 663584 | tf_op jit(solution)/shard_map/while/body/eval_jaxpr/ppermute | solution.py:9
  302.3 3.9 fusion.9
  308.1 16.9 %collective-permute-done = f32[2304,72]{0,1:T(8,128)S(1)} collective-permute-done((f32[2304,72]{0,1:T(8,128)}, f32[2304,72]{0,1:T(8,128)S(1)}, u32[]{:S(2)}, u32[]{:S(2)}) %collective-permute-start) | collective-permute-done | bytes 663584 | tf_op jit(solution)/shard_map/while/body/eval_jaxpr/ppermute | solution.py:9
  324.9 3.9 fusion.9
  328.8 1.9 collective-permute-start
  330.7 16.9 %collective-permute-done = f32[2304,72]{0,1:T(8,128)S(1)} collective-permute-done((f32[2304,72]{0,1:T(8,128)}, f32[2304,72]{0,1:T(8,128)S(1)}, u32[]{:S(2)}, u32[]{:S(2)}) %collective-permute-start) | collective-permute-done | bytes 663584 | tf_op jit(solution)/shard_map/while/body/eval_jaxpr/ppermute | solution.py:9
  347.6 3.9 fusion.9
  353.4 16.9 %collective-permute-done = f32[2304,72]{0,1:T(8,128)S(1)} collective-permute-done((f32[2304,72]{0,1:T(8,128)}, f32[2304,72]{0,1:T(8,128)S(1)}, u32[]{:S(2)}, u32[]{:S(2)}) %collective-permute-start) | collective-permute-done | bytes 663584 | tf_op jit(solution)/shard_map/while/body/eval_jaxpr/ppermute | solution.py:9
  370.2 3.9 fusion.9
  374.1 1.9 collective-permute-start
  376.0 16.9 %collective-permute-done = f32[2304,72]{0,1:T(8,128)S(1)} collective-permute-done((f32[2304,72]{0,1:T(8,128)}, f32[2304,72]{0,1:T(8,128)S(1)}, u32[]{:S(2)}, u32[]{:S(2)}) %collective-permute-start) | collective-permute-done | bytes 663584 | tf_op jit(solution)/shard_map/while/body/eval_jaxpr/ppermute | solution.py:9
  392.9 3.9 fusion.9
  396.8 1.9 collective-permute-start
  398.7 16.9 %collective-permute-done = f32[2304,72]{0,1:T(8,128)S(1)} collective-permute-done((f32[2304,72]{0,1:T(8,128)}, f32[2304,72]{0,1:T(8,128)S(1)}, u32[]{:S(2)}, u32[]{:S(2)}) %collective-permute-start) | collective-permute-done | bytes 663584 | tf_op jit(solution)/shard_map/while/body/eval_jaxpr/ppermute | solution.py:9
  415.5 3.9 fusion.9
  419.4 1.9 collective-permute-start
  421.3 16.9 %collective-permute-done = f32[2304,72]{0,1:T(8,128)S(1)} collective-permute-done((f32[2304,72]{0,1:T(8,128)}, f32[2304,72]{0,1:T(8,128)S(1)}, u32[]{:S(2)}, u32[]{:S(2)}) %collective-permute-start) | collective-permute-done | bytes 663584 | tf_op jit(solution)/shard_map/while/body/eval_jaxpr/ppermute | solution.py:9
  438.2 3.9 fusion.9
  444.0 16.9 %collective-permute-done = f32[2304,72]{0,1:T(8,128)S(1)} collective-permute-done((f32[2304,72]{0,1:T(8,128)}, f32[2304,72]{0,1:T(8,128)S(1)}, u32[]{:S(2)}, u32[]{:S(2)}) %collective-permute-start) | collective-permute-done | bytes 663584 | tf_op jit(solution)/shard_map/while/body/eval_jaxpr/ppermute | solution.py:9
  462.3 23.5 %reduce-scatter.4.cloned.1.call-done = f32[576,72]{1,0:T(8,128)} async-done(((f32[2304,72]{1,0:T(8,128)}), f32[576,72]{1,0:T(8,128)}) %reduce-scatter.4.cloned.1.call-update) | async-done | bytes 165904
  (12 shorter events, 12.8 us)
Async XLA Ops:
  8.8 62.3 %copy-start = (f32[2304,288]{0,1:T(8,128)S(1)}, f32[2304,288]{0,1:T(8,128)}, u32[]{:S(2)}) copy-start(f32[2304,288]{0,1:T(8,128)} %param.4) | copy-start | bytes 7962628
  8.8 62.2 %all-to-all-start = ((f32[8,288,144]{1,2,0:T(8,128)}), f32[8,288,144]{1,2,0:T(8,128)}, u32[]{:S(2)}, u32[]{:S(2)}) async-start(f32[8,288,144]{1,2,0:T(8,128)} %stack.2), calls=%async_computation | async-start | bytes 3538944 | tf_op jit(solution)/shard_map/all_to_all | solution.py:14
  27.2 458.6 %reduce-scatter.4.cloned.1.call-start = ((), (), s32[]{:S(2)}) async-start(), calls=%async_computation.2 | async-start | bytes 1474560
  75.0 46.1 %collective-permute-start = (f32[2304,72]{0,1:T(8,128)}, f32[2304,72]{0,1:T(8,128)S(1)}, u32[]{:S(2)}, u32[]{:S(2)}) collective-permute-start(f32[2304,72]{0,1:T(8,128)} %fusion.9), channel_id=1, source_target_pairs={{0,4},{4,8},{8,12},{12,16},{16,20},{20,24},{24,28},{28,32},{32,36}... | collective-permute-start | bytes 1990664 | tf_op jit(solution)/shard_map/while/body/eval_jaxpr/ppermute | solution.py:9
  124.9 18.8 %collective-permute-start = (f32[2304,72]{0,1:T(8,128)}, f32[2304,72]{0,1:T(8,128)S(1)}, u32[]{:S(2)}, u32[]{:S(2)}) collective-permute-start(f32[2304,72]{0,1:T(8,128)} %fusion.9), channel_id=1, source_target_pairs={{0,4},{4,8},{8,12},{12,16},{16,20},{20,24},{24,28},{28,32},{32,36}... | collective-permute-start | bytes 1990664 | tf_op jit(solution)/shard_map/while/body/eval_jaxpr/ppermute | solution.py:9
  147.6 18.8 %collective-permute-start = (f32[2304,72]{0,1:T(8,128)}, f32[2304,72]{0,1:T(8,128)S(1)}, u32[]{:S(2)}, u32[]{:S(2)}) collective-permute-start(f32[2304,72]{0,1:T(8,128)} %fusion.9), channel_id=1, source_target_pairs={{0,4},{4,8},{8,12},{12,16},{16,20},{20,24},{24,28},{28,32},{32,36}... | collective-permute-start | bytes 1990664 | tf_op jit(solution)/shard_map/while/body/eval_jaxpr/ppermute | solution.py:9
  170.2 18.8 %collective-permute-start = (f32[2304,72]{0,1:T(8,128)}, f32[2304,72]{0,1:T(8,128)S(1)}, u32[]{:S(2)}, u32[]{:S(2)}) collective-permute-start(f32[2304,72]{0,1:T(8,128)} %fusion.9), channel_id=1, source_target_pairs={{0,4},{4,8},{8,12},{12,16},{16,20},{20,24},{24,28},{28,32},{32,36}... | collective-permute-start | bytes 1990664 | tf_op jit(solution)/shard_map/while/body/eval_jaxpr/ppermute | solution.py:9
  192.9 18.8 %collective-permute-start = (f32[2304,72]{0,1:T(8,128)}, f32[2304,72]{0,1:T(8,128)S(1)}, u32[]{:S(2)}, u32[]{:S(2)}) collective-permute-start(f32[2304,72]{0,1:T(8,128)} %fusion.9), channel_id=1, source_target_pairs={{0,4},{4,8},{8,12},{12,16},{16,20},{20,24},{24,28},{28,32},{32,36}... | collective-permute-start | bytes 1990664 | tf_op jit(solution)/shard_map/while/body/eval_jaxpr/ppermute | solution.py:9
  215.5 18.8 %collective-permute-start = (f32[2304,72]{0,1:T(8,128)}, f32[2304,72]{0,1:T(8,128)S(1)}, u32[]{:S(2)}, u32[]{:S(2)}) collective-permute-start(f32[2304,72]{0,1:T(8,128)} %fusion.9), channel_id=1, source_target_pairs={{0,4},{4,8},{8,12},{12,16},{16,20},{20,24},{24,28},{28,32},{32,36}... | collective-permute-start | bytes 1990664 | tf_op jit(solution)/shard_map/while/body/eval_jaxpr/ppermute | solution.py:9
  238.2 18.8 %collective-permute-start = (f32[2304,72]{0,1:T(8,128)}, f32[2304,72]{0,1:T(8,128)S(1)}, u32[]{:S(2)}, u32[]{:S(2)}) collective-permute-start(f32[2304,72]{0,1:T(8,128)} %fusion.9), channel_id=1, source_target_pairs={{0,4},{4,8},{8,12},{12,16},{16,20},{20,24},{24,28},{28,32},{32,36}... | collective-permute-start | bytes 1990664 | tf_op jit(solution)/shard_map/while/body/eval_jaxpr/ppermute | solution.py:9
  260.8 18.8 %collective-permute-start = (f32[2304,72]{0,1:T(8,128)}, f32[2304,72]{0,1:T(8,128)S(1)}, u32[]{:S(2)}, u32[]{:S(2)}) collective-permute-start(f32[2304,72]{0,1:T(8,128)} %fusion.9), channel_id=1, source_target_pairs={{0,4},{4,8},{8,12},{12,16},{16,20},{20,24},{24,28},{28,32},{32,36}... | collective-permute-start | bytes 1990664 | tf_op jit(solution)/shard_map/while/body/eval_jaxpr/ppermute | solution.py:9
  283.5 18.8 %collective-permute-start = (f32[2304,72]{0,1:T(8,128)}, f32[2304,72]{0,1:T(8,128)S(1)}, u32[]{:S(2)}, u32[]{:S(2)}) collective-permute-start(f32[2304,72]{0,1:T(8,128)} %fusion.9), channel_id=1, source_target_pairs={{0,4},{4,8},{8,12},{12,16},{16,20},{20,24},{24,28},{28,32},{32,36}... | collective-permute-start | bytes 1990664 | tf_op jit(solution)/shard_map/while/body/eval_jaxpr/ppermute | solution.py:9
  306.1 18.8 %collective-permute-start = (f32[2304,72]{0,1:T(8,128)}, f32[2304,72]{0,1:T(8,128)S(1)}, u32[]{:S(2)}, u32[]{:S(2)}) collective-permute-start(f32[2304,72]{0,1:T(8,128)} %fusion.9), channel_id=1, source_target_pairs={{0,4},{4,8},{8,12},{12,16},{16,20},{20,24},{24,28},{28,32},{32,36}... | collective-permute-start | bytes 1990664 | tf_op jit(solution)/shard_map/while/body/eval_jaxpr/ppermute | solution.py:9
  328.8 18.8 %collective-permute-start = (f32[2304,72]{0,1:T(8,128)}, f32[2304,72]{0,1:T(8,128)S(1)}, u32[]{:S(2)}, u32[]{:S(2)}) collective-permute-start(f32[2304,72]{0,1:T(8,128)} %fusion.9), channel_id=1, source_target_pairs={{0,4},{4,8},{8,12},{12,16},{16,20},{20,24},{24,28},{28,32},{32,36}... | collective-permute-start | bytes 1990664 | tf_op jit(solution)/shard_map/while/body/eval_jaxpr/ppermute | solution.py:9
  351.4 18.8 %collective-permute-start = (f32[2304,72]{0,1:T(8,128)}, f32[2304,72]{0,1:T(8,128)S(1)}, u32[]{:S(2)}, u32[]{:S(2)}) collective-permute-start(f32[2304,72]{0,1:T(8,128)} %fusion.9), channel_id=1, source_target_pairs={{0,4},{4,8},{8,12},{12,16},{16,20},{20,24},{24,28},{28,32},{32,36}... | collective-permute-start | bytes 1990664 | tf_op jit(solution)/shard_map/while/body/eval_jaxpr/ppermute | solution.py:9
  374.1 18.8 %collective-permute-start = (f32[2304,72]{0,1:T(8,128)}, f32[2304,72]{0,1:T(8,128)S(1)}, u32[]{:S(2)}, u32[]{:S(2)}) collective-permute-start(f32[2304,72]{0,1:T(8,128)} %fusion.9), channel_id=1, source_target_pairs={{0,4},{4,8},{8,12},{12,16},{16,20},{20,24},{24,28},{28,32},{32,36}... | collective-permute-start | bytes 1990664 | tf_op jit(solution)/shard_map/while/body/eval_jaxpr/ppermute | solution.py:9
  396.8 18.8 %collective-permute-start = (f32[2304,72]{0,1:T(8,128)}, f32[2304,72]{0,1:T(8,128)S(1)}, u32[]{:S(2)}, u32[]{:S(2)}) collective-permute-start(f32[2304,72]{0,1:T(8,128)} %fusion.9), channel_id=1, source_target_pairs={{0,4},{4,8},{8,12},{12,16},{16,20},{20,24},{24,28},{28,32},{32,36}... | collective-permute-start | bytes 1990664 | tf_op jit(solution)/shard_map/while/body/eval_jaxpr/ppermute | solution.py:9
  419.4 18.8 %collective-permute-start = (f32[2304,72]{0,1:T(8,128)}, f32[2304,72]{0,1:T(8,128)S(1)}, u32[]{:S(2)}, u32[]{:S(2)}) collective-permute-start(f32[2304,72]{0,1:T(8,128)} %fusion.9), channel_id=1, source_target_pairs={{0,4},{4,8},{8,12},{12,16},{16,20},{20,24},{24,28},{28,32},{32,36}... | collective-permute-start | bytes 1990664 | tf_op jit(solution)/shard_map/while/body/eval_jaxpr/ppermute | solution.py:9
  442.1 18.8 %collective-permute-start = (f32[2304,72]{0,1:T(8,128)}, f32[2304,72]{0,1:T(8,128)S(1)}, u32[]{:S(2)}, u32[]{:S(2)}) collective-permute-start(f32[2304,72]{0,1:T(8,128)} %fusion.9), channel_id=1, source_target_pairs={{0,4},{4,8},{8,12},{12,16},{16,20},{20,24},{24,28},{28,32},{32,36}... | collective-permute-start | bytes 1990664 | tf_op jit(solution)/shard_map/while/body/eval_jaxpr/ppermute | solution.py:9
Sparse Core Ops, SparseCore 0:
  462.4 23.3 reduce-scatter.3
